TPU v7x, 32 devices: a whole 2x2x4 slice. The times are simulated.
32 devices in a mesh: row: 4 (over y, x), col: 8 (over z, core).
Axes of the slice: x: 2, y: 2, z: 4, core: 2. Of those that a mesh axis runs over, the one named last changes fastest.
Arguments:
- amplitude: float32 [32, 80, 5, 640], P('col', 'row'), may hold values from -6 to 6
- coupling: float32 [80, 5, 32, 640], P('row', None, 'col'), may hold values from -0.3125 to 0.3125
Outputs:
- cycle_term: float32 [32, 640, 32, 640], P('row', None, 'col')
All inputs are finite; a program needn't handle non-finite values.
Results may differ from a plain program's by a relative error of at most 0.00005.
Values sent between devices are 32-bit elements; how exact they have to be, the bound alone decides.
A program may use at most 192 MiB of HBM per device.

v0:
```python
import jax
import jax.numpy as jnp
from jax import lax
from jax.sharding import PartitionSpec as P


def shards(amplitude, coupling):
    all_rows = lax.all_gather(amplitude, "row", axis=1, tiled=True)
    whole_pairs = lax.all_gather(amplitude, "col", axis=0, tiled=True)
    panel = lax.all_to_all(whole_pairs, "row", split_axis=0, concat_axis=1, tiled=True)
    coupling_panel = lax.all_gather(coupling, "row", axis=0, tiled=True)
    widened = lax.all_gather(coupling, "col", axis=2, tiled=True)
    complete = lax.all_to_all(widened, "row", split_axis=2, concat_axis=0, tiled=True)
    own_rows = panel.shape[0]
    own_cols = all_rows.shape[0]
    summed = panel.shape[1] * panel.shape[2]
    width = panel.shape[3]
    panel_flat = jnp.transpose(panel.reshape(own_rows, summed, width), (1, 0, 2)).reshape(
        summed, own_rows * width
    )
    complete_flat = complete.reshape(summed, own_rows * width)
    coupling_flat = coupling_panel.reshape(summed, own_cols * width)
    rows_flat = jnp.transpose(all_rows.reshape(own_cols, summed, width), (1, 0, 2)).reshape(
        summed, own_cols * width
    )
    left = jnp.concatenate([panel_flat, complete_flat], axis=0)
    right = jnp.concatenate([coupling_flat, rows_flat], axis=0)
    result = lax.dot_general(
        left,
        right,
        (((0,), (0,)), ((), ())),
        precision=lax.Precision.HIGHEST,
        preferred_element_type=jnp.float32,
    )
    return result.reshape(own_rows, width, own_cols, width)


def solution(mesh):
    placed = (P("col", "row", None, None), P("row", None, "col", None))
    return jax.shard_map(
        shards, mesh=mesh, in_specs=placed, out_specs=P("row", None, "col", None), check_vma=False
    )
```

profile of v0, /device:TPU:7, one launch (start us, length us, event | category | flops | bytes accessed | tf_op | source)
XLA Modules:
  0.0 669.8 jit_solution(1339903822620963579)
XLA Ops:
  6.5 0.0 all-gather.5.cloned.1.call-start
  6.5 2.3 copy.13
  8.9 0.0 all-gather.5.cloned.1.call-update
  8.9 0.0 all-gather.7.cloned.1.call-start
  8.9 2.3 copy.16
  11.3 0.0 all-gather.7.cloned.1.call-update
  11.3 0.0 all-gather.11.cloned.1.call-start
  11.4 0.7 all-gather.11.cloned.1.call-update
  12.1 92.6 %all-gather.5.cloned.1.call-done = f32[32,20,5,640]{3,1,2,0:T(8,128)} async-done(((f32[4,20,5,640]{3,1,2,0:T(8,128)}), f32[32,20,5,640]{3,1,2,0:T(8,128)}) %all-gather.5.cloned.1.call-update) | async-done | bytes 8192016 | tf_op jit(solution)/shard_map/all_gather | solution.py:9
  104.6 6.1 all-to-all-start
  110.7 0.0 all-gather.9.cloned.1.call-start
  110.7 0.6 all-gather.9.cloned.1.call-update
  111.3 87.5 %all-gather.7.cloned.1.call-done = f32[20,5,32,640]{3,0,1,2:T(8,128)} async-done(((f32[20,5,4,640]{3,0,1,2:T(8,128)}), f32[20,5,32,640]{3,0,1,2:T(8,128)}) %all-gather.7.cloned.1.call-update) | async-done | bytes 8192016 | tf_op jit(solution)/shard_map/all_gather | solution.py:12
  198.7 27.4 %all-to-all-done = f32[32,20,5,640]{3,1,2,0:T(8,128)} async-done(((f32[32,20,5,640]{3,1,2,0:T(8,128)}), f32[32,20,5,640]{3,1,2,0:T(8,128)}, u32[]{:S(2)}, u32[]{:S(2)}) %all-to-all-start) | async-done | bytes 8192032 | tf_op jit(solution)/shard_map/all_to_all | solution.py:10
  226.2 6.7 all-to-all-start.1
  232.9 43.7 %all-gather.11.cloned.1.call-done = f32[4,80,5,640]{3,0,2,1:T(4,128)} async-done(((f32[4,20,5,640]{3,0,2,1:T(4,128)}), f32[4,80,5,640]{3,0,2,1:T(4,128)}) %all-gather.11.cloned.1.call-update) | async-done | bytes 4096016 | tf_op jit(solution)/shard_map/all_gather | solution.py:8
  276.5 4.4 copy.22
  280.9 118.5 %all-gather.9.cloned.1.call-done = f32[80,5,4,640]{3,2,1,0:T(4,128)} async-done(((f32[20,5,4,640]{3,2,1,0:T(4,128)}), f32[80,5,4,640]{3,2,1,0:T(4,128)}) %all-gather.9.cloned.1.call-update) | async-done | bytes 4096016 | tf_op jit(solution)/shard_map/all_gather | solution.py:11
  399.4 0.0 copy-start
  399.4 2.6 copy.21
  402.0 0.8 copy-done
  402.8 3.8 fusion.14
  406.6 5.2 copy.15
  411.9 4.9 copy.19
  416.8 0.0 all-to-all-done.1
  416.8 5.2 copy.17
  422.1 0.0 copy-start.1
  422.1 5.2 copy.20
  427.2 0.0 copy-done.1
  427.2 175.6 %fusion = f32[5120,2560]{1,0:T(8,128)} fusion(f32[400,5120]{1,0:T(8,128)} %bitcast.27, f32[400,5120]{1,0:T(8,128)S(1)} %bitcast.26, f32[800,2560]{1,0:T(8,128)} %fusion.14), kind=kOutput, calls=%fused_computation | convolution fusion | flops 125833216000 | bytes 77004800 | tf_op jit(solution)/shard_map/dot_general | solution.py:28
  602.9 60.4 %reshape.29 = f32[8,640,4,640]{3,2,1,0:T(4,128)} reshape(f32[5120,2560]{1,0:T(8,128)} %fusion) | data formatting | bytes 104857600 | tf_op jit(solution)/shard_map/reshape | solution.py:35
Async XLA Ops:
  6.5 98.1 %all-gather.5.cloned.1.call-start = ((), (), s32[]{:S(2)}) async-start(), calls=%async_computation.2 | async-start | bytes 11059200 | tf_op jit(solution)/shard_map/all_gather | solution.py:9
  8.9 189.8 %all-gather.7.cloned.1.call-start = ((), (), s32[]{:S(2)}) async-start(), calls=%async_computation.3 | async-start | bytes 11059200 | tf_op jit(solution)/shard_map/all_gather | solution.py:12
  11.3 265.2 %all-gather.11.cloned.1.call-start = ((), (), s32[]{:S(2)}) async-start(), calls=%async_computation.5 | async-start | bytes 5120000 | tf_op jit(solution)/shard_map/all_gather | solution.py:8
  104.6 121.5 %all-to-all-start = ((f32[32,20,5,640]{3,1,2,0:T(8,128)}), f32[32,20,5,640]{3,1,2,0:T(8,128)}, u32[]{:S(2)}, u32[]{:S(2)}) async-start(f32[32,20,5,640]{3,1,2,0:T(8,128)} %all-gather.5.cloned.1.call-done), calls=%async_computation | async-start | bytes 19660800 | tf_op jit(solution)/shard_map/all_to_all | solution.py:10
  110.7 288.7 %all-gather.9.cloned.1.call-start = ((), (), s32[]{:S(2)}) async-start(), calls=%async_computation.4 | async-start | bytes 5120000 | tf_op jit(solution)/shard_map/all_gather | solution.py:11
  226.2 190.7 %all-to-all-start.1 = ((f32[20,5,32,640]{3,0,1,2:T(8,128)}), f32[20,5,32,640]{3,0,1,2:T(8,128)}, u32[]{:S(2)}, u32[]{:S(2)}) async-start(f32[20,5,32,640]{3,0,1,2:T(8,128)} %all-gather.7.cloned.1.call-done), calls=%async_computation.1 | async-start | bytes 19660800 | tf_op jit(solution)/shard_map/all_to_all | solution.py:13
  399.4 3.4 copy-start
  422.1 5.2 copy-start.1
Sparse Core Ops, SparseCore 0:
  9.0 95.5 all-gather.4
  106.3 92.3 all-gather.6
  200.6 75.9 all-gather.10
  278.2 121.1 all-gather.8
where the time goes:
time: 674 us; the launch traced here: 670 us
  waiting for transfers between devices  371 us (55%)
  matrix products  176 us (26%)
  local copies, waits for them, and re-layouts  93.4 us (14%)
  between operations  13.1 us (2%)
  starting transfers between devices  12.8 us (2%)
    dot_general x1, matrix products, shards(): lax.dot_general(left, right, (((0,), (0,)), ((), ())), precision=lax.Prec...  176 us
    all_gather x1, waiting for transfers between devices, shards(): coupling_panel = lax.all_gather(coupling, 'row', axis=0, tiled=True)  118 us
    all_gather x1, waiting for transfers between devices, shards(): whole_pairs = lax.all_gather(amplitude, 'col', axis=0, tiled=True)  92.6 us
    all_gather x1, waiting for transfers between devices, shards(): widened = lax.all_gather(coupling, 'col', axis=2, tiled=True)  87.5 us
    reshape x1, local copies, waits for them, and re-layouts, shards(): return result.reshape(own_rows, width, own_cols, width)  60.4 us
    all_gather x1, waiting for transfers between devices, shards(): all_rows = lax.all_gather(amplitude, 'row', axis=1, tiled=True)  43.7 us
    all_to_all x1, waiting for transfers between devices, shards(): lax.all_to_all(whole_pairs, 'row', split_axis=0, concat_axis=1, tiled=True)  27.4 us
    unnamed x10, local copies, waits for them, and re-layouts  22.6 us
  transfers between devices with their start and end apart: 6, of which 5 were waited for; matrix products, arithmetic and copies ran while one was open for 3% of the time, Pallas kernels for 0%

commit v1 on v0

v1 whole, which is shorter than its diff:
```python
import functools

import jax
import jax.numpy as jnp
from jax import lax
from jax.experimental import pallas as pl
from jax.experimental.pallas import tpu as pltpu
from jax.sharding import PartitionSpec as P

MESH = pl.DeviceIdType.MESH


def gather_kernel(
    rows, parts, s_ref, right_ref, left_ref,
    own_sem, row_send, row_recv, up_send, down_send, chain_recv, side_send, side_recv, keep_sem,
):
    r = lax.axis_index("row")
    col = lax.axis_index("col")
    q = col // 2
    c = col % 2
    sibling = 2 * q + 1 - c
    above = lax.rem(col + 2, 2 * rows)
    below = lax.rem(col + 2 * rows - 2, 2 * rows)
    is_source = q == r
    goes_up = jnp.logical_and(q >= r, q < rows - 1)
    goes_down = jnp.logical_and(q <= r, q > 0)

    def origin(t):
        return lax.rem(r - t + rows, rows)

    barrier = pltpu.get_barrier_semaphore()
    for t in range(1, rows):
        pl.semaphore_signal(barrier, inc=1, device_id=(lax.rem(r + t, rows), col), device_id_type=MESH)
    for other in (above, below, sibling):
        pl.semaphore_signal(barrier, inc=1, device_id=(r, other), device_id_type=MESH)
    pl.semaphore_wait(barrier, rows + 2)

    def row_copy(t, p):
        return pltpu.make_async_remote_copy(
            src_ref=s_ref.at[p], dst_ref=right_ref.at[r, p],
            send_sem=row_send.at[t, p], recv_sem=row_recv.at[t, p],
            device_id=(lax.rem(r + t, rows), col), device_id_type=MESH,
        )

    def row_arrival(t, p):
        return pltpu.make_async_remote_copy(
            src_ref=s_ref.at[p], dst_ref=right_ref.at[origin(t), p],
            send_sem=row_send.at[t, p], recv_sem=row_recv.at[t, p],
            device_id=(lax.rem(r + t, rows), col), device_id_type=MESH,
        )

    def chain_copy(src, t, p, sem, target, arrival):
        return pltpu.make_async_remote_copy(
            src_ref=src, dst_ref=left_ref.at[c, origin(t), p],
            send_sem=sem.at[t, p], recv_sem=arrival.at[t, p],
            device_id=(r, target), device_id_type=MESH,
        )

    def side_arrival(t, p):
        return pltpu.make_async_remote_copy(
            src_ref=s_ref.at[p], dst_ref=left_ref.at[1 - c, origin(t), p],
            send_sem=side_send.at[t, p], recv_sem=side_recv.at[t, p],
            device_id=(r, sibling), device_id_type=MESH,
        )

    def keep_copy(src, t, p):
        return pltpu.make_async_copy(src, left_ref.at[c, origin(t), p], keep_sem.at[t, p])

    def forward(src, t, p):
        @pl.when(goes_up)
        def _():
            chain_copy(src, t, p, up_send, above, chain_recv).start()

        @pl.when(goes_down)
        def _():
            chain_copy(src, t, p, down_send, below, chain_recv).start()

        chain_copy(src, t, p, side_send, sibling, side_recv).start()

    def step(t, p, first):
        @pl.when(is_source)
        def _():
            if first:
                src = s_ref.at[p]
            else:
                row_arrival(t, p).wait_recv()
                src = right_ref.at[origin(t), p]
            forward(src, t, p)
            keep_copy(src, t, p).start()

        @pl.when(jnp.logical_not(is_source))
        def _():
            src = left_ref.at[c, origin(t), p]
            chain_copy(src, t, p, up_send, above, chain_recv).wait_recv()
            forward(src, t, p)

    own = pltpu.make_async_copy(s_ref, right_ref.at[r], own_sem)
    own.start()

    def send_rows(p, carry):
        for t in range(1, rows):
            row_copy(t, p).start()
        return carry

    lax.fori_loop(0, parts, send_rows, 0)

    def first_step(p, carry):
        step(0, p, True)
        return carry

    lax.fori_loop(0, parts, first_step, 0)

    def later_step(n, carry):
        step(1 + lax.rem(n, rows - 1), n // (rows - 1), False)
        return carry

    lax.fori_loop(0, parts * (rows - 1), later_step, 0)

    own.wait()

    def finish_rows(n, carry):
        t = 1 + lax.rem(n, rows - 1)
        p = n // (rows - 1)
        row_copy(t, p).wait_send()

        @pl.when(jnp.logical_not(is_source))
        def _():
            row_arrival(t, p).wait_recv()

        return carry

    lax.fori_loop(0, parts * (rows - 1), finish_rows, 0)

    def finish_chain(n, carry):
        t = lax.rem(n, rows)
        p = n // rows
        src = s_ref.at[p]

        @pl.when(goes_up)
        def _():
            chain_copy(src, t, p, up_send, above, chain_recv).wait_send()

        @pl.when(goes_down)
        def _():
            chain_copy(src, t, p, down_send, below, chain_recv).wait_send()

        chain_copy(src, t, p, side_send, sibling, side_recv).wait_send()
        side_arrival(t, p).wait_recv()

        @pl.when(is_source)
        def _():
            keep_copy(src, t, p).wait()

        return carry

    lax.fori_loop(0, parts * rows, finish_chain, 0)


def gather(s, rows):
    parts, depth, width = s.shape
    sems = pltpu.SemaphoreType.DMA((rows, parts))
    return pl.pallas_call(
        functools.partial(gather_kernel, rows, parts),
        out_shape=(
            jax.ShapeDtypeStruct((rows, parts, depth, width), s.dtype),
            jax.ShapeDtypeStruct((2, rows, parts, depth, width), s.dtype),
        ),
        in_specs=[pl.BlockSpec(memory_space=pl.ANY)],
        out_specs=[pl.BlockSpec(memory_space=pl.ANY)] * 2,
        scratch_shapes=[pltpu.SemaphoreType.DMA] + [sems] * 8,
        compiler_params=pltpu.CompilerParams(collective_id=0, has_side_effects=True),
    )(s)


def split(x):
    high = x.astype(jnp.bfloat16)
    low = (x - high.astype(jnp.float32)).astype(jnp.bfloat16)
    return high, low


def product_kernel(rows, parts, depth, width, right_ref, left_ref, out_ref, flat, rhs, lhs):
    total = rows * depth
    body = total // 128 * 128
    rest = total - body
    padded = rhs.shape[0]
    half = depth // 2

    @pl.when(pl.program_id(0) == 0)
    def _():
        if padded > 3 * total:
            rhs[3 * total :, :] = jnp.zeros((padded - 3 * total, parts * width), jnp.bfloat16)
        for j in range(parts):
            for k in range(rows):
                flat[k * depth : k * depth + half, :] = right_ref[k, j, half:, :]
                flat[k * depth + half : (k + 1) * depth, :] = right_ref[k, j, :half, :]
            high, low = split(flat[...])
            cols = slice(j * width, (j + 1) * width)
            rhs[:body, cols] = high[:body]
            rhs[body : 2 * body, cols] = high[:body]
            rhs[2 * body : 3 * body, cols] = low[:body]
            if rest:
                base = 3 * body
                rhs[base : base + rest, cols] = high[body:]
                rhs[base + rest : base + 2 * rest, cols] = high[body:]
                rhs[base + 2 * rest : base + 3 * rest, cols] = low[body:]

    for k in range(rows):
        flat[k * depth : (k + 1) * depth, :] = left_ref[0, k, 0]
    for at in range(0, body, 128):
        high, low = split(flat[at : at + 128, :].T)
        lhs[:, at : at + 128] = high
        lhs[:, body + at : body + at + 128] = low
        lhs[:, 2 * body + at : 2 * body + at + 128] = high
    if rest:
        x = flat[body:, :]
        high = x.astype(jnp.bfloat16).astype(jnp.float32)
        pieces = [high, x - high, high]
        if padded > 3 * total:
            pieces.append(jnp.zeros((padded - 3 * total, width), jnp.float32))
        lhs[:, 3 * body :] = jnp.concatenate(pieces, axis=0).T.astype(jnp.bfloat16)

    blocks = width // 128
    for n in range(0, parts * blocks, 2):
        result = jnp.dot(lhs[...], rhs[:, n * 128 : (n + 2) * 128], preferred_element_type=jnp.float32)
        for h in range(2):
            j, b = divmod(n + h, blocks)
            out_ref[0, :, j, b * 128 : (b + 1) * 128] = result[:, h * 128 : (h + 1) * 128]


def product(right, left):
    rows, parts, depth, width = right.shape
    total = rows * depth
    padded = -(-3 * total // 128) * 128
    own_rows = 2 * parts
    return pl.pallas_call(
        functools.partial(product_kernel, rows, parts, depth, width),
        grid=(own_rows,),
        out_shape=jax.ShapeDtypeStruct((own_rows, width, parts, width), jnp.float32),
        in_specs=[
            pl.BlockSpec((rows, parts, depth, width), lambda i: (0, 0, 0, 0), pipeline_mode=pl.Buffered(1)),
            pl.BlockSpec((1, rows, 1, depth, width), lambda i: (i // parts, 0, i % parts, 0, 0)),
        ],
        out_specs=pl.BlockSpec((1, width, parts, width), lambda i: (i, 0, 0, 0)),
        scratch_shapes=[
            pltpu.VMEM((total, width), jnp.float32),
            pltpu.VMEM((padded, parts * width), jnp.bfloat16),
            pltpu.VMEM((width, padded), jnp.bfloat16),
        ],
        compiler_params=pltpu.CompilerParams(vmem_limit_bytes=58 * 1024 * 1024),
        cost_estimate=pl.CostEstimate(
            flops=2 * padded * own_rows * width * parts * width,
            bytes_accessed=4 * own_rows * width * parts * width,
            transcendentals=0,
        ),
    )(right, left)


def solution(mesh):
    rows = mesh.shape["row"]

    def shards(amplitude, coupling):
        parts, occupied, block, width = amplitude.shape
        depth = occupied * block
        mine = jnp.concatenate(
            [
                amplitude.reshape(parts, depth, width),
                jnp.transpose(coupling.reshape(depth, parts, width), (1, 0, 2)),
            ],
            axis=1,
        )
        right, left = gather(mine, rows)
        return product(right, left)

    placed = (P("col", "row", None, None), P("row", None, "col", None))
    return jax.shard_map(
        shards, mesh=mesh, in_specs=placed, out_specs=P("row", None, "col", None), check_vma=False
    )
```

time: 674 us -> 423 us (0.63)
  the two profiles are of different devices: /device:TPU:7 before, /device:TPU:0 now
where the time goes in v1:
time: 423 us
  Pallas kernels  420 us (99%)
    pallas_call x1, Pallas kernels, gather(): pl.pallas_call(functools.partial(gather_kernel, rows, parts), out_shape=(...  318 us
    pallas_call x1, Pallas kernels, product(): pl.pallas_call(functools.partial(product_kernel, rows, parts, depth, widt...  102 us

profile of v1, /device:TPU:0, one launch (start us, length us, event | category | flops | bytes accessed | tf_op | source)
XLA Modules:
  0.0 422.6 jit_solution(8244900232015030796)
XLA Ops:
  0.0 0.0 copy-start
  0.0 1.4 copy.6
  1.4 0.1 copy-done
  1.5 0.1 copy.8
  1.6 1.4 pad_maximum_fusion.s_ref
  3.0 317.5 %shard_map.28 = (f32[4,4,200,640]{3,2,1,0:T(8,128)}, f32[2,4,4,200,640]{4,3,2,1,0:T(8,128)}) custom-call(f32[4,200,640]{2,1,0:T(8,128)} %pad_maximum_fusion.s_ref), custom_call_target="tpu_custom_call" | custom-call | tf_op jit(solution)/shard_map/pallas_call | solution.py:162
  320.5 102.0 %shard_map.29 = f32[8,640,4,640]{3,2,1,0:T(4,128)} custom-call(f32[4,4,200,640]{3,2,1,0:T(8,128)} %get-tuple-element.7.right_ref, f32[2,4,4,200,640]{4,3,2,1,0:T(8,128)} %get-tuple-element.8.left_ref), custom_call_target="tpu_custom_call" | custom-call | flops 63753420800 | bytes 52428800 | tf_op jit(solution)/shard_map/pallas_call | solution.py:235
Async XLA Ops:
  0.0 1.5 copy-start

commit v2 on v1

--- a/solution.py
+++ b/solution.py
@@ -12,7 +12,7 @@
 
 def gather_kernel(
     rows, parts, s_ref, right_ref, left_ref,
-    own_sem, row_send, row_recv, up_send, down_send, chain_recv, side_send, side_recv, keep_sem,
+    own_sem, row_send, row_recv, up_send, down_send, chain_recv, side_send, side_recv,
 ):
     r = lax.axis_index("row")
     col = lax.axis_index("col")
@@ -63,9 +63,6 @@
             device_id=(r, sibling), device_id_type=MESH,
         )
 
-    def keep_copy(src, t, p):
-        return pltpu.make_async_copy(src, left_ref.at[c, origin(t), p], keep_sem.at[t, p])
-
     def forward(src, t, p):
         @pl.when(goes_up)
         def _():
@@ -86,7 +83,6 @@
                 row_arrival(t, p).wait_recv()
                 src = right_ref.at[origin(t), p]
             forward(src, t, p)
-            keep_copy(src, t, p).start()
 
         @pl.when(jnp.logical_not(is_source))
         def _():
@@ -146,11 +142,6 @@
 
         chain_copy(src, t, p, side_send, sibling, side_recv).wait_send()
         side_arrival(t, p).wait_recv()
-
-        @pl.when(is_source)
-        def _():
-            keep_copy(src, t, p).wait()
-
         return carry
 
     lax.fori_loop(0, parts * rows, finish_chain, 0)
@@ -167,7 +158,7 @@
         ),
         in_specs=[pl.BlockSpec(memory_space=pl.ANY)],
         out_specs=[pl.BlockSpec(memory_space=pl.ANY)] * 2,
-        scratch_shapes=[pltpu.SemaphoreType.DMA] + [sems] * 8,
+        scratch_shapes=[pltpu.SemaphoreType.DMA] + [sems] * 7,
         compiler_params=pltpu.CompilerParams(collective_id=0, has_side_effects=True),
     )(s)
 
@@ -178,15 +169,17 @@
     return high, low
 
 
-def product_kernel(rows, parts, depth, width, right_ref, left_ref, out_ref, flat, rhs, lhs):
+def product_kernel(rows, parts, depth, width, right_ref, left_ref, out_ref, flat, rhs, even, odd):
     total = rows * depth
     body = total // 128 * 128
     rest = total - body
     padded = rhs.shape[0]
     half = depth // 2
-
-    @pl.when(pl.program_id(0) == 0)
-    def _():
+    step = pl.program_id(0)
+    q = lax.axis_index("col") // 2
+    c = lax.axis_index("col") % 2
+
+    def prepare_right():
         if padded > 3 * total:
             rhs[3 * total :, :] = jnp.zeros((padded - 3 * total, parts * width), jnp.bfloat16)
         for j in range(parts):
@@ -204,27 +197,66 @@
                 rhs[base + rest : base + 2 * rest, cols] = high[body:]
                 rhs[base + 2 * rest : base + 3 * rest, cols] = low[body:]
 
-    for k in range(rows):
-        flat[k * depth : (k + 1) * depth, :] = left_ref[0, k, 0]
-    for at in range(0, body, 128):
-        high, low = split(flat[at : at + 128, :].T)
-        lhs[:, at : at + 128] = high
-        lhs[:, body + at : body + at + 128] = low
-        lhs[:, 2 * body + at : 2 * body + at + 128] = high
-    if rest:
-        x = flat[body:, :]
-        high = x.astype(jnp.bfloat16).astype(jnp.float32)
-        pieces = [high, x - high, high]
-        if padded > 3 * total:
-            pieces.append(jnp.zeros((padded - 3 * total, width), jnp.float32))
-        lhs[:, 3 * body :] = jnp.concatenate(pieces, axis=0).T.astype(jnp.bfloat16)
-
+    def prepare_chunk(lhs, at):
+        if at < body:
+            high, low = split(flat[at : at + 128, :].T)
+            lhs[:, at : at + 128] = high
+            lhs[:, body + at : body + at + 128] = low
+            lhs[:, 2 * body + at : 2 * body + at + 128] = high
+        elif rest:
+            x = flat[body:, :]
+            high = x.astype(jnp.bfloat16).astype(jnp.float32)
+            pieces = [high, x - high, high]
+            if padded > 3 * total:
+                pieces.append(jnp.zeros((padded - 3 * total, width), jnp.float32))
+            lhs[:, 3 * body :] = jnp.concatenate(pieces, axis=0).T.astype(jnp.bfloat16)
+
+    chunks = list(range(0, body + 1, 128))
     blocks = width // 128
-    for n in range(0, parts * blocks, 2):
-        result = jnp.dot(lhs[...], rhs[:, n * 128 : (n + 2) * 128], preferred_element_type=jnp.float32)
-        for h in range(2):
-            j, b = divmod(n + h, blocks)
-            out_ref[0, :, j, b * 128 : (b + 1) * 128] = result[:, h * 128 : (h + 1) * 128]
+
+    def multiply(lhs, following):
+        pending = list(chunks)
+        for n in range(0, parts * blocks, 2):
+            result = jnp.dot(lhs[...], rhs[:, n * 128 : (n + 2) * 128], preferred_element_type=jnp.float32)
+            take = -(-len(chunks) * 2 // (parts * blocks))
+            for at in pending[:take]:
+                prepare_chunk(following, at)
+            pending = pending[take:]
+            for h in range(2):
+                j, b = divmod(n + h, blocks)
+                out_ref[0, :, j, b * 128 : (b + 1) * 128] = result[:, h * 128 : (h + 1) * 128]
+        for at in pending:
+            prepare_chunk(following, at)
+
+    @pl.when(step == 0)
+    def _():
+        prepare_right()
+
+    index = jnp.minimum(step, 2 * parts - 1)
+    from_right = jnp.logical_and(q == lax.axis_index("row"), index // parts == c)
+
+    @pl.when(from_right)
+    def _():
+        for k in range(rows):
+            flat[k * depth : (k + 1) * depth, :] = right_ref[k, lax.rem(index, parts)]
+
+    @pl.when(jnp.logical_not(from_right))
+    def _():
+        for k in range(rows):
+            flat[k * depth : (k + 1) * depth, :] = left_ref[0, k, 0]
+
+    @pl.when(step == 0)
+    def _():
+        for at in chunks:
+            prepare_chunk(even, at)
+
+    @pl.when(step % 2 == 1)
+    def _():
+        multiply(even, odd)
+
+    @pl.when(jnp.logical_and(step % 2 == 0, step > 0))
+    def _():
+        multiply(odd, even)
 
 
 def product(right, left):
@@ -232,18 +264,24 @@
     total = rows * depth
     padded = -(-3 * total // 128) * 128
     own_rows = 2 * parts
+
+    def left_block(step):
+        i = jnp.minimum(step, own_rows - 1)
+        return i // parts, 0, i % parts, 0, 0
+
     return pl.pallas_call(
         functools.partial(product_kernel, rows, parts, depth, width),
-        grid=(own_rows,),
+        grid=(own_rows + 1,),
         out_shape=jax.ShapeDtypeStruct((own_rows, width, parts, width), jnp.float32),
         in_specs=[
             pl.BlockSpec((rows, parts, depth, width), lambda i: (0, 0, 0, 0), pipeline_mode=pl.Buffered(1)),
-            pl.BlockSpec((1, rows, 1, depth, width), lambda i: (i // parts, 0, i % parts, 0, 0)),
+            pl.BlockSpec((1, rows, 1, depth, width), left_block),
         ],
-        out_specs=pl.BlockSpec((1, width, parts, width), lambda i: (i, 0, 0, 0)),
+        out_specs=pl.BlockSpec((1, width, parts, width), lambda i: (jnp.maximum(i - 1, 0), 0, 0, 0)),
         scratch_shapes=[
             pltpu.VMEM((total, width), jnp.float32),
             pltpu.VMEM((padded, parts * width), jnp.bfloat16),
+            pltpu.VMEM((width, padded), jnp.bfloat16),
             pltpu.VMEM((width, padded), jnp.bfloat16),
         ],
         compiler_params=pltpu.CompilerParams(vmem_limit_bytes=58 * 1024 * 1024),

time: 423 us -> 315 us (0.74)
  the two profiles are of different devices: /device:TPU:0 before, /device:TPU:7 now
where the time goes in v2:
time: 315 us; the launch traced here: 314 us
  Pallas kernels  311 us (99%)
    pallas_call x1, Pallas kernels, gather(): pl.pallas_call(functools.partial(gather_kernel, rows, parts), out_shape=(...  208 us
    pallas_call x1, Pallas kernels, product(): pl.pallas_call(functools.partial(product_kernel, rows, parts, depth, widt...  103 us

profile of v2, /device:TPU:7, one launch (start us, length us, event | category | flops | bytes accessed | tf_op | source)
XLA Modules:
  0.0 314.5 jit_solution(8875243865222505480)
XLA Ops:
  0.0 0.0 copy-start
  0.0 1.4 copy.6
  1.4 0.1 copy-done
  1.5 0.1 copy.8
  1.6 1.4 pad_maximum_fusion.s_ref
  3.0 208.0 %shard_map.28 = (f32[4,4,200,640]{3,2,1,0:T(8,128)}, f32[2,4,4,200,640]{4,3,2,1,0:T(8,128)}) custom-call(f32[4,200,640]{2,1,0:T(8,128)} %pad_maximum_fusion.s_ref), custom_call_target="tpu_custom_call" | custom-call | tf_op jit(solution)/shard_map/pallas_call | solution.py:153
  211.1 103.4 %shard_map.29 = f32[8,640,4,640]{3,2,1,0:T(4,128)} custom-call(f32[4,4,200,640]{3,2,1,0:T(8,128)} %get-tuple-element.7.right_ref, f32[2,4,4,200,640]{4,3,2,1,0:T(8,128)} %get-tuple-element.8.left_ref), custom_call_target="tpu_custom_call" | custom-call | flops 63753420800 | bytes 52428800 | tf_op jit(solution)/shard_map/pallas_call | solution.py:272
Async XLA Ops:
  0.0 1.5 copy-start

commit v3 on v2

--- a/solution.py
+++ b/solution.py
@@ -169,12 +169,13 @@
     return high, low
 
 
-def product_kernel(rows, parts, depth, width, right_ref, left_ref, out_ref, flat, rhs, even, odd):
+def product_kernel(rows, parts, depth, width, right_ref, left_ref, out_ref, flat, rhs, even, odd, woven):
     total = rows * depth
     body = total // 128 * 128
     rest = total - body
     padded = rhs.shape[0]
     half = depth // 2
+    blocks = width // 128
     step = pl.program_id(0)
     q = lax.axis_index("col") // 2
     c = lax.axis_index("col") % 2
@@ -187,15 +188,17 @@
                 flat[k * depth : k * depth + half, :] = right_ref[k, j, half:, :]
                 flat[k * depth + half : (k + 1) * depth, :] = right_ref[k, j, :half, :]
             high, low = split(flat[...])
-            cols = slice(j * width, (j + 1) * width)
-            rhs[:body, cols] = high[:body]
-            rhs[body : 2 * body, cols] = high[:body]
-            rhs[2 * body : 3 * body, cols] = low[:body]
-            if rest:
-                base = 3 * body
-                rhs[base : base + rest, cols] = high[body:]
-                rhs[base + rest : base + 2 * rest, cols] = high[body:]
-                rhs[base + 2 * rest : base + 3 * rest, cols] = low[body:]
+            for b in range(blocks):
+                piece = slice(b * 128, (b + 1) * 128)
+                cols = slice((b * parts + j) * 128, (b * parts + j + 1) * 128)
+                rhs[:body, cols] = high[:body, piece]
+                rhs[body : 2 * body, cols] = high[:body, piece]
+                rhs[2 * body : 3 * body, cols] = low[:body, piece]
+                if rest:
+                    base = 3 * body
+                    rhs[base : base + rest, cols] = high[body:, piece]
+                    rhs[base + rest : base + 2 * rest, cols] = high[body:, piece]
+                    rhs[base + 2 * rest : base + 3 * rest, cols] = low[body:, piece]
 
     def prepare_chunk(lhs, at):
         if at < body:
@@ -212,21 +215,21 @@
             lhs[:, 3 * body :] = jnp.concatenate(pieces, axis=0).T.astype(jnp.bfloat16)
 
     chunks = list(range(0, body + 1, 128))
-    blocks = width // 128
 
     def multiply(lhs, following):
         pending = list(chunks)
-        for n in range(0, parts * blocks, 2):
-            result = jnp.dot(lhs[...], rhs[:, n * 128 : (n + 2) * 128], preferred_element_type=jnp.float32)
-            take = -(-len(chunks) * 2 // (parts * blocks))
+        take = -(-len(chunks) // blocks)
+        for b in range(blocks):
+            mixed = woven.at[b % 2]
+            for n in range(0, parts, 2):
+                at = (b * parts + n) * 128
+                result = jnp.dot(lhs[...], rhs[:, at : at + 256], preferred_element_type=jnp.float32)
+                for h in range(2):
+                    mixed[pl.ds(n + h, width, stride=parts), :] = result[:, h * 128 : (h + 1) * 128]
             for at in pending[:take]:
                 prepare_chunk(following, at)
             pending = pending[take:]
-            for h in range(2):
-                j, b = divmod(n + h, blocks)
-                out_ref[0, :, j, b * 128 : (b + 1) * 128] = result[:, h * 128 : (h + 1) * 128]
-        for at in pending:
-            prepare_chunk(following, at)
+            out_ref[0, :, :, b * 128 : (b + 1) * 128] = mixed[...].reshape(width, parts, 128)
 
     @pl.when(step == 0)
     def _():
@@ -283,6 +286,7 @@
             pltpu.VMEM((padded, parts * width), jnp.bfloat16),
             pltpu.VMEM((width, padded), jnp.bfloat16),
             pltpu.VMEM((width, padded), jnp.bfloat16),
+            pltpu.VMEM((2, width * parts, 128), jnp.float32),
         ],
         compiler_params=pltpu.CompilerParams(vmem_limit_bytes=58 * 1024 * 1024),
         cost_estimate=pl.CostEstimate(

time: 315 us -> 299 us (0.949)
  Pallas kernels: 311 us -> 296 us
    pallas_call x1, Pallas kernels: 103 us -> 88.1 us  [product(): pl.pallas_call(functools.partial(product_kernel, rows, parts, depth, widt...]
where the time goes in v3:
time: 299 us
  Pallas kernels  296 us (99%)
    pallas_call x1, Pallas kernels, gather(): pl.pallas_call(functools.partial(gather_kernel, rows, parts), out_shape=(...  208 us
    pallas_call x1, Pallas kernels, product(): pl.pallas_call(functools.partial(product_kernel, rows, parts, depth, widt...  88.1 us

profile of v3, /device:TPU:7, one launch (start us, length us, event | category | flops | bytes accessed | tf_op | source)
XLA Modules:
  0.0 299.1 jit_solution(14470172681736228462)
XLA Ops:
  0.0 0.0 copy-start
  0.0 1.4 copy.6
  1.4 0.1 copy-done
  1.5 0.1 copy.8
  1.6 1.4 pad_maximum_fusion.s_ref
  3.0 208.0 %shard_map.28 = (f32[4,4,200,640]{3,2,1,0:T(8,128)}, f32[2,4,4,200,640]{4,3,2,1,0:T(8,128)}) custom-call(f32[4,200,640]{2,1,0:T(8,128)} %pad_maximum_fusion.s_ref), custom_call_target="tpu_custom_call" | custom-call | tf_op jit(solution)/shard_map/pallas_call | solution.py:153
  211.1 88.1 %shard_map.29 = f32[8,640,4,640]{3,2,1,0:T(4,128)} custom-call(f32[4,4,200,640]{3,2,1,0:T(8,128)} %get-tuple-element.7.right_ref, f32[2,4,4,200,640]{4,3,2,1,0:T(8,128)} %get-tuple-element.8.left_ref), custom_call_target="tpu_custom_call" | custom-call | flops 63753420800 | bytes 52428800 | tf_op jit(solution)/shard_map/pallas_call | solution.py:275
Async XLA Ops:
  0.0 1.5 copy-start
